TPU v7x, 256 devices: a whole 4x4x8 slice. The times are simulated.
256 devices in a mesh: sec: 16 (over z, core), op: 16 (over x, y).
Axes of the slice: x: 4, y: 4, z: 8, core: 2. Of those that a mesh axis runs over, the one named last changes fastest.
Arguments:
- theta: float32 [32, 512, 512], P('sec', 'op'), may hold values from -6 to 6
- counts: int32 [32], P('sec'), may hold values from 256 to 512, as said below
- pair_source: int32 [256], P('sec'), may hold values from 0 to 1
- pair_target: int32 [256], P('sec'), may hold values from 0 to 31
- left_ops: float32 [1024, 512, 512], P(('sec', 'op')), may hold values from -0.25 to 0.25
- right_ops: float32 [1024, 512, 512], P(('sec', 'op')), may hold values from -0.25 to 0.25
Outputs:
- cheb_last: float32 [32, 512, 512], P('sec', 'op')
- cheb_prev: float32 [32, 512, 512], P('sec', 'op')
Inputs may be any that keep to these rules, and one draw needn't show every extreme that they name: `counts`: every sector has between 256 and 512 live states; some sector has exactly 512 and some exactly 256.
All inputs are finite; a program needn't handle non-finite values.
Results may differ from a plain program's by a relative error of at most 0.0001.
Values sent between devices are 32-bit elements; how exact they have to be, the bound alone decides.
A program may use at most 64 MiB of HBM per device.

v0:
```python
import math
import jax
import jax.numpy as jnp
from jax import lax
from jax.sharding import PartitionSpec as P

STEPS = 3


def per_device(theta, counts, pair_source, pair_target, left_ops, right_ops):
    op_count = lax.axis_size("op")
    op_place = lax.axis_index("op")
    sec_place = lax.axis_index("sec")
    sec_local = theta.shape[0]
    row_count = theta.shape[1]
    order_size = theta.shape[2]
    pairs_local = left_ops.shape[0]
    group_blocks = pair_target.shape[0]
    sectors_all = sec_local * lax.axis_size("sec")
    factor = 0.5 / math.sqrt(group_blocks * pairs_local / sec_local)
    highest = lax.Precision.HIGHEST
    my_source = lax.dynamic_index_in_dim(pair_source, op_place, 0, keepdims=False)
    row_numbers = op_place * row_count + jnp.arange(row_count, dtype=jnp.int32)
    row_alive = row_numbers[None, :] < counts[:, None]
    column_alive = jnp.arange(order_size, dtype=jnp.int32)[None, :] < counts[:, None]
    live_mask = (row_alive[:, :, None] & column_alive[:, None, :]).astype(jnp.float32)
    target_hot = (pair_target[None, :] == jnp.arange(sectors_all, dtype=jnp.int32)[:, None]).astype(
        jnp.float32
    )

    def hamiltonian(iterate):
        gathered = lax.all_gather(iterate, "op", axis=1, tiled=True)
        chosen = lax.dynamic_index_in_dim(gathered, my_source, 0, keepdims=False)
        left_product = jnp.einsum("pmr,rn->pmn", left_ops, chosen, precision=highest)
        block_term = jnp.einsum("pmk,pnk->mn", left_product, right_ops, precision=highest)
        split_rows = block_term.reshape(op_count, row_count, order_size)
        block_rows = lax.all_to_all(split_rows, "op", split_axis=0, concat_axis=0, tiled=True)
        flat_rows = block_rows.reshape(group_blocks, row_count * order_size)
        sector_sums = jnp.dot(
            target_hot, flat_rows, precision=highest, preferred_element_type=jnp.float32
        )
        sector_sums = sector_sums.reshape(sectors_all, row_count, order_size)
        whole_sums = lax.psum(sector_sums, "sec")
        own_sums = lax.dynamic_slice_in_dim(whole_sums, sec_place * sec_local, sec_local, 0)
        return factor * own_sums * live_mask

    previous = theta * live_mask
    current = hamiltonian(previous)
    for step_number in range(STEPS - 1):
        following = 2.0 * hamiltonian(current) - previous
        previous, current = (current, following)
    return (current, previous)


def solution(mesh):
    in_specs = (
        P("sec", "op", None),
        P("sec"),
        P("sec"),
        P("sec"),
        P(("sec", "op"), None, None),
        P(("sec", "op"), None, None),
    )
    out_specs = (P("sec", "op", None), P("sec", "op", None))
    return jax.shard_map(
        per_device, mesh=mesh, in_specs=in_specs, out_specs=out_specs, check_vma=False
    )
```

profile of v0, /device:TPU:1, one launch (start us, length us, event | category | flops | bytes accessed | tf_op | source)
XLA Modules:
  0.0 675.0 jit_solution(8471230393268469698)
XLA Ops:
  7.2 0.0 all-gather.4.cloned.1.call-start
  7.2 0.7 iota_compare_fusion.1
  8.0 0.7 broadcast_compare_fusion
  8.7 1.7 and_select_fusion.3
  10.4 0.0 all-gather.4.cloned.1.call-update
  10.4 0.0 all-reduce.4.cloned.1.call-start
  10.5 1.2 dynamic_slice.23
  13.7 50.3 %all-gather.4.cloned.1.call-done = f32[2,512,512]{2,0,1:T(2,128)} async-done(((f32[2,32,512]{2,0,1:T(2,128)}), f32[2,512,512]{2,0,1:T(2,128)}) %all-gather.4.cloned.1.call-update) | async-done | bytes 2097168 | tf_op jit(solution)/shard_map/all_gather | solution.py:32
  63.9 2.5 constant_dynamic-slice_fusion.2
  66.4 1.3 copy.18
  67.8 0.0 copy-start
  67.8 10.3 %fusion.19 = f32[512,4,512]{2,0,1:T(8,128)S(1)} fusion(f32[4,512,512]{2,1,0:T(8,128)} %param.10, f32[1,512,512]{1,2,0:T(8,128)S(1)} %copy.18), kind=kOutput, calls=%fused_computation.19 | convolution fusion | flops 6442450944 | bytes 9437184 | tf_op jit(solution)/shard_map/pmr,rn->pmn/dot_general | solution.py:34
  78.1 0.0 copy-done
  78.1 0.0 copy-start.5
  78.1 13.9 %fusion.4 = f32[512,512,1]{1,0,2:T(8,128)S(1)} fusion(f32[4,512,512]{2,1,0:T(8,128)S(1)} %copy-done, f32[512,4,512]{2,0,1:T(8,128)S(1)} %fusion.19), kind=kOutput, calls=%fused_computation.4 | convolution fusion | flops 6442450944 | bytes 9437184 | tf_op jit(solution)/shard_map/pmk,pnk->mn/dot_general | solution.py:35
  92.0 19.3 %all_to_all.15 = f32[16,32,512]{2,1,0:T(8,128)S(1)} all-to-all(f32[16,32,512]{2,1,0:T(8,128)S(1)} %bitcast.75), channel_id=1, replica_groups=mesh['sec'=16,'op'=16] {'op'}, dimensions={0} | all-to-all | bytes 2097152 | tf_op jit(solution)/shard_map/all_to_all | solution.py:37
  111.3 0.0 copy-done.5
  111.3 2.9 fusion.12
  114.2 0.0 all-reduce.4.cloned.1.call-update
  114.2 0.0 all-gather.6.cloned.1.call-start
  114.2 115.1 %all-reduce.4.cloned.1.call-done = f32[32,32,512]{2,0,1:T(8,128)} async-done(((f32[32,32,512]{2,0,1:T(8,128)}), f32[32,32,512]{2,0,1:T(8,128)}) %all-reduce.4.cloned.1.call-update) | async-done | bytes 2097168 | tf_op jit(solution)/shard_map/psum | solution.py:43
  229.4 1.8 and_select_fusion.2
  231.2 0.0 all-gather.6.cloned.1.call-update
  231.3 0.0 all-reduce.6.cloned.1.call-start
  231.3 50.7 %all-gather.6.cloned.1.call-done = f32[2,512,512]{2,0,1:T(2,128)} async-done(((f32[2,32,512]{2,0,1:T(2,128)}), f32[2,512,512]{2,0,1:T(2,128)}) %all-gather.6.cloned.1.call-update) | async-done | bytes 2097168 | tf_op jit(solution)/shard_map/all_gather | solution.py:32
  282.0 2.5 constant_dynamic-slice_fusion.1
  284.5 1.3 copy.21
  285.8 0.0 copy-start.1
  285.8 10.3 %fusion.17 = f32[512,4,512]{2,0,1:T(8,128)S(1)} fusion(f32[4,512,512]{2,1,0:T(8,128)} %param.10, f32[1,512,512]{1,2,0:T(8,128)S(1)} %copy.21), kind=kOutput, calls=%fused_computation.17 | convolution fusion | flops 6442450944 | bytes 9437184 | tf_op jit(solution)/shard_map/pmr,rn->pmn/dot_general | solution.py:34
  296.1 0.0 copy-done.1
  296.1 13.7 %fusion.2 = f32[512,512,1]{1,0,2:T(8,128)S(1)} fusion(f32[4,512,512]{2,1,0:T(8,128)S(1)} %copy-done.1, f32[512,4,512]{2,0,1:T(8,128)S(1)} %fusion.17), kind=kOutput, calls=%fused_computation.2 | convolution fusion | flops 6442450944 | bytes 9437184 | tf_op jit(solution)/shard_map/pmk,pnk->mn/dot_general | solution.py:35
  309.8 0.0 copy-start.4
  309.9 19.4 %all_to_all.16 = f32[16,32,512]{2,1,0:T(8,128)S(1)} all-to-all(f32[16,32,512]{2,1,0:T(8,128)S(1)} %bitcast.76), channel_id=1, replica_groups=mesh['sec'=16,'op'=16] {'op'}, dimensions={0} | all-to-all | bytes 2097152 | tf_op jit(solution)/shard_map/all_to_all | solution.py:37
  329.2 2.9 fusion.9
  332.1 0.0 all-reduce.6.cloned.1.call-update
  332.2 0.0 all-gather.8.cloned.1.call-start
  332.2 115.3 %all-reduce.6.cloned.1.call-done = f32[32,32,512]{2,0,1:T(8,128)} async-done(((f32[32,32,512]{2,0,1:T(8,128)}), f32[32,32,512]{2,0,1:T(8,128)}) %all-reduce.6.cloned.1.call-update) | async-done | bytes 2097168 | tf_op jit(solution)/shard_map/psum | solution.py:43
  447.5 0.0 copy-done.4
  447.5 1.9 fusion.22
  449.5 0.0 all-gather.8.cloned.1.call-update
  449.5 0.0 all-reduce.8.cloned.1.call-start
  449.5 50.4 %all-gather.8.cloned.1.call-done = f32[2,512,512]{2,0,1:T(2,128)} async-done(((f32[2,32,512]{2,0,1:T(2,128)}), f32[2,512,512]{2,0,1:T(2,128)}) %all-gather.8.cloned.1.call-update) | async-done | bytes 2097168 | tf_op jit(solution)/shard_map/all_gather | solution.py:32
  500.0 2.5 constant_dynamic-slice_fusion
  502.5 1.3 copy.24
  503.8 0.0 copy-start.2
  503.8 10.3 %fusion.15 = f32[512,4,512]{2,0,1:T(8,128)S(1)} fusion(f32[4,512,512]{2,1,0:T(8,128)} %param.10, f32[1,512,512]{1,2,0:T(8,128)S(1)} %copy.24), kind=kOutput, calls=%fused_computation.15 | convolution fusion | flops 6442450944 | bytes 9437184 | tf_op jit(solution)/shard_map/pmr,rn->pmn/dot_general | solution.py:34
  514.1 0.0 copy-done.2
  514.1 13.8 %fusion = f32[512,512,1]{1,0,2:T(8,128)S(1)} fusion(f32[4,512,512]{2,1,0:T(8,128)S(1)} %copy-done.2, f32[512,4,512]{2,0,1:T(8,128)S(1)} %fusion.15), kind=kOutput, calls=%fused_computation | convolution fusion | flops 6442450944 | bytes 9437184 | tf_op jit(solution)/shard_map/pmk,pnk->mn/dot_general | solution.py:35
  528.0 0.0 copy-start.3
  528.0 19.4 %all_to_all.17 = f32[16,32,512]{2,1,0:T(8,128)S(1)} all-to-all(f32[16,32,512]{2,1,0:T(8,128)S(1)} %bitcast.77), channel_id=1, replica_groups=mesh['sec'=16,'op'=16] {'op'}, dimensions={0} | all-to-all | bytes 2097152 | tf_op jit(solution)/shard_map/all_to_all | solution.py:37
  547.4 2.9 fusion.6
  550.3 0.0 all-reduce.8.cloned.1.call-update
  550.3 0.0 copy-done.3
  550.3 0.7 copy.28
  551.0 114.5 %all-reduce.8.cloned.1.call-done = f32[32,32,512]{2,0,1:T(8,128)} async-done(((f32[32,32,512]{2,0,1:T(8,128)}), f32[32,32,512]{2,0,1:T(8,128)}) %all-reduce.8.cloned.1.call-update) | async-done | bytes 2097168 | tf_op jit(solution)/shard_map/psum | solution.py:43
  665.5 1.4 fusion.24
  666.9 0.7 copy.27
  (1 shorter events, 0.0 us)
Async XLA Ops:
  7.2 56.8 %all-gather.4.cloned.1.call-start = ((), (), s32[]{:S(2)}) async-start(), calls=%async_computation.3 | async-start | bytes 2228224 | tf_op jit(solution)/shard_map/all_gather | solution.py:32
  10.4 219.0 %all-reduce.4.cloned.1.call-start = ((), (), s32[]{:S(2)}) async-start(), calls=%async_computation.4 | async-start | bytes 4194304 | tf_op jit(solution)/shard_map/psum | solution.py:43
  67.8 10.3 %copy-start = (f32[4,512,512]{2,1,0:T(8,128)S(1)}, f32[4,512,512]{2,1,0:T(8,128)}, u32[]{:S(2)}) copy-start(f32[4,512,512]{2,1,0:T(8,128)} %param.11) | copy-start | bytes 12582916
  78.1 33.2 %copy-start.5 = (s32[16]{0:T(128)S(1)}, s32[16]{0:T(128)}, u32[]{:S(2)}) copy-start(s32[16]{0:T(128)} %param.9) | copy-start | bytes 196
  114.2 167.8 %all-gather.6.cloned.1.call-start = ((), (), s32[]{:S(2)}) async-start(), calls=%async_computation.5 | async-start | bytes 2228224 | tf_op jit(solution)/shard_map/all_gather | solution.py:32
  231.3 216.3 %all-reduce.6.cloned.1.call-start = ((), (), s32[]{:S(2)}) async-start(), calls=%async_computation.6 | async-start | bytes 4194304 | tf_op jit(solution)/shard_map/psum | solution.py:43
  285.8 10.3 %copy-start.1 = (f32[4,512,512]{2,1,0:T(8,128)S(1)}, f32[4,512,512]{2,1,0:T(8,128)}, u32[]{:S(2)}) copy-start(f32[4,512,512]{2,1,0:T(8,128)} %param.11) | copy-start | bytes 12582916
  309.8 137.7 %copy-start.4 = (f32[2,32,512]{2,1,0:T(8,128)S(1)}, f32[2,32,512]{2,1,0:T(8,128)}, u32[]{:S(2)}) copy-start(f32[2,32,512]{2,1,0:T(8,128)} %param.6) | copy-start | bytes 393220
  332.2 167.8 %all-gather.8.cloned.1.call-start = ((), (), s32[]{:S(2)}) async-start(), calls=%async_computation.7 | async-start | bytes 2228224 | tf_op jit(solution)/shard_map/all_gather | solution.py:32
  449.5 216.0 %all-reduce.8.cloned.1.call-start = ((), (), s32[]{:S(2)}) async-start(), calls=%async_computation.8 | async-start | bytes 4194304 | tf_op jit(solution)/shard_map/psum | solution.py:43
  503.8 10.4 %copy-start.2 = (f32[4,512,512]{2,1,0:T(8,128)S(1)}, f32[4,512,512]{2,1,0:T(8,128)}, u32[]{:S(2)}) copy-start(f32[4,512,512]{2,1,0:T(8,128)} %param.11) | copy-start | bytes 12582916
  528.0 22.3 %copy-start.3 = (f32[2,32,512]{2,0,1:T(2,128)S(1)}, f32[2,32,512]{2,0,1:T(2,128)}, u32[]{:S(2)}) copy-start(f32[2,32,512]{2,0,1:T(2,128)} %fusion.22) | copy-start | bytes 393220
Sparse Core Ops, SparseCore 0:
  11.0 52.8 all-gather.3
  114.3 115.0 all-reduce.3
  232.4 49.5 all-gather.5
  332.3 115.2 all-reduce.5
  450.4 49.5 all-gather.7
  550.4 115.0 all-reduce.7
where the time goes:
time: 680 us; the launch traced here: 675 us
  waiting for transfers between devices  496 us (73%)
  matrix products  81 us (12%)
  blocking collectives  58 us (9%)
  between operations  16.7 us (2%)
  local copies, waits for them, and re-layouts  14 us (2%)
  other arithmetic  8.39 us (1%)
    psum x3, waiting for transfers between devices, hamiltonian(): whole_sums = lax.psum(sector_sums, 'sec')  345 us
    all_gather x3, waiting for transfers between devices, hamiltonian(): gathered = lax.all_gather(iterate, 'op', axis=1, tiled=True)  151 us
    all_to_all x3, blocking collectives, hamiltonian(): lax.all_to_all(split_rows, 'op', split_axis=0, concat_axis=0, tiled=True)  58 us
    dot_general x3, matrix products, hamiltonian(): jnp.einsum('pmk,pnk->mn', left_product, right_ops, precision=highest)  41.5 us
    dot_general x3, matrix products, hamiltonian(): jnp.einsum('pmr,rn->pmn', left_ops, chosen, precision=highest)  30.9 us
  transfers between devices with their start and end apart: 6, of which 6 were waited for; matrix products, arithmetic and copies ran while one was open for 0% of the time, Pallas kernels for 0%

commit v1 on v0

--- a/solution.py
+++ b/solution.py
@@ -5,6 +5,14 @@
 from jax.sharding import PartitionSpec as P
 
 STEPS = 3
+
+
+def add_in_pairs(x, axis):
+    count, total = (lax.axis_size(axis), x)
+    for far in [1 << k for k in range(count.bit_length() - 1)]:
+        swap = [(i, i ^ far) for i in range(count)]
+        total = total + lax.ppermute(total, axis, swap)
+    return total
 
 
 def per_device(theta, counts, pair_source, pair_target, left_ops, right_ops):
@@ -40,7 +48,7 @@
             target_hot, flat_rows, precision=highest, preferred_element_type=jnp.float32
         )
         sector_sums = sector_sums.reshape(sectors_all, row_count, order_size)
-        whole_sums = lax.psum(sector_sums, "sec")
+        whole_sums = add_in_pairs(sector_sums, "sec")
         own_sums = lax.dynamic_slice_in_dim(whole_sums, sec_place * sec_local, sec_local, 0)
         return factor * own_sums * live_mask
 

time: 680 us -> 1050 us (1.54)
  waiting for transfers between devices: 496 us -> 830 us
  starting transfers between devices: 0.25 us -> 40.9 us
    ppermute x0 -> x12, waiting for transfers between devices: none -> 690 us  [add_in_pairs(): total = total + lax.ppermute(total, axis, swap)]
    psum x3 -> x0, waiting for transfers between devices: 345 us -> none  [hamiltonian(): whole_sums = lax.psum(sector_sums, 'sec')]
    ppermute x0 -> x12, starting transfers between devices: none -> 40.7 us  [add_in_pairs(): total = total + lax.ppermute(total, axis, swap)]
    all_gather x3, waiting for transfers between devices: 151 us -> 140 us  [hamiltonian(): gathered = lax.all_gather(iterate, 'op', axis=1, tiled=True)]
  transfers between devices with their start and end apart: 6 -> 15, of which waited for: 6 -> 15; matrix products, arithmetic and copies ran while one was open for 0% -> 0% of each run, Pallas kernels for 0% -> 0%
where the time goes in v1:
time: 1050 us
  waiting for transfers between devices  830 us (79%)
  matrix products  77.2 us (7%)
  blocking collectives  57.8 us (6%)
  starting transfers between devices  40.9 us (4%)
  between operations  16.2 us (2%)
  local copies, waits for them, and re-layouts  14 us (1%)
  other arithmetic  11.6 us (1%)
    ppermute x12, waiting for transfers between devices, add_in_pairs(): total = total + lax.ppermute(total, axis, swap)  690 us
    all_gather x3, waiting for transfers between devices, hamiltonian(): gathered = lax.all_gather(iterate, 'op', axis=1, tiled=True)  140 us
    all_to_all x3, blocking collectives, hamiltonian(): lax.all_to_all(split_rows, 'op', split_axis=0, concat_axis=0, tiled=True)  57.8 us
    dot_general x3, matrix products, hamiltonian(): jnp.einsum('pmk,pnk->mn', left_product, right_ops, precision=highest)  41.4 us
    ppermute x12, starting transfers between devices, add_in_pairs(): total = total + lax.ppermute(total, axis, swap)  40.7 us
    dot_general x3, matrix products, hamiltonian(): jnp.einsum('pmr,rn->pmn', left_ops, chosen, precision=highest)  31.1 us
  transfers between devices with their start and end apart: 15, of which 15 were waited for; matrix products, arithmetic and copies ran while one was open for 0% of the time, Pallas kernels for 0%

profile of v1, /device:TPU:1, one launch (start us, length us, event | category | flops | bytes accessed | tf_op | source)
XLA Modules:
  0.0 1048.0 jit_solution(14944196980539690806)
XLA Ops:
  7.2 0.7 iota_compare_fusion.1
  8.0 0.7 broadcast_compare_fusion
  8.7 1.7 and_select_fusion.3
  10.4 0.0 all-gather.6.cloned.1.call-start
  10.5 1.2 dynamic_slice.23
  13.7 50.3 %all-gather.4.cloned.1.call-done = f32[2,512,512]{2,0,1:T(2,128)} async-done(((f32[2,32,512]{2,0,1:T(2,128)}), f32[2,512,512]{2,0,1:T(2,128)}) %all-gather.4.cloned.1.call-update) | async-done | bytes 2097168 | tf_op jit(solution)/shard_map/all_gather | solution.py:40
  63.9 2.5 constant_dynamic-slice_fusion.2
  66.4 1.3 copy.18
  67.8 10.5 %fusion.19 = f32[512,4,512]{2,0,1:T(8,128)S(1)} fusion(f32[4,512,512]{2,1,0:T(8,128)} %param.10, f32[1,512,512]{1,2,0:T(8,128)S(1)} %copy.18), kind=kOutput, calls=%fused_computation.19 | convolution fusion | flops 6442450944 | bytes 9437184 | tf_op jit(solution)/shard_map/pmr,rn->pmn/dot_general | solution.py:42
  78.3 13.7 %fusion.4 = f32[512,512,1]{1,0,2:T(8,128)S(1)} fusion(f32[4,512,512]{2,1,0:T(8,128)S(1)} %copy-done, f32[512,4,512]{2,0,1:T(8,128)S(1)} %fusion.19), kind=kOutput, calls=%fused_computation.4 | convolution fusion | flops 6442450944 | bytes 9437184 | tf_op jit(solution)/shard_map/pmk,pnk->mn/dot_general | solution.py:43
  92.1 19.3 %all_to_all.15 = f32[16,32,512]{2,1,0:T(8,128)S(1)} all-to-all(f32[16,32,512]{2,1,0:T(8,128)S(1)} %bitcast.75), channel_id=1, replica_groups=mesh['sec'=16,'op'=16] {'op'}, dimensions={0} | all-to-all | bytes 2097152 | tf_op jit(solution)/shard_map/all_to_all | solution.py:45
  111.3 1.6 fusion.12
  112.9 3.3 collective-permute-start
  116.2 3.8 collective-permute-done
  120.0 0.6 add.65
  120.7 1.4 collective-permute-start.1
  122.0 45.6 %collective-permute-done.1 = f32[32,32,512]{2,0,1:T(8,128)S(1)} collective-permute-done((f32[32,32,512]{2,0,1:T(8,128)S(1)}, f32[32,32,512]{2,0,1:T(8,128)S(1)}, u32[]{:S(2)}, u32[]{:S(2)}) %collective-permute-start.1) | collective-permute-done | bytes 2097184 | tf_op jit(solution)/shard_map/ppermute | solution.py:14
  167.6 0.6 add.66
  168.2 2.4 collective-permute-start.2
  170.6 90.1 %collective-permute-done.2 = f32[32,32,512]{2,0,1:T(8,128)S(1)} collective-permute-done((f32[32,32,512]{2,0,1:T(8,128)S(1)}, f32[32,32,512]{2,0,1:T(8,128)S(1)}, u32[]{:S(2)}, u32[]{:S(2)}) %collective-permute-start.2) | collective-permute-done | bytes 2097184 | tf_op jit(solution)/shard_map/ppermute | solution.py:14
  260.6 0.5 add.67
  261.1 6.5 collective-permute-start.3
  267.6 90.8 %collective-permute-done.3 = f32[32,32,512]{2,0,1:T(8,128)} collective-permute-done((f32[32,32,512]{2,0,1:T(8,128)S(1)}, f32[32,32,512]{2,0,1:T(8,128)}, u32[]{:S(2)}, u32[]{:S(2)}) %collective-permute-start.3) | collective-permute-done | bytes 2097184 | tf_op jit(solution)/shard_map/ppermute | solution.py:14
  358.5 1.9 and_select_fusion.2
  360.4 45.1 %all-gather.6.cloned.1.call-done = f32[2,512,512]{2,0,1:T(2,128)} async-done(((f32[2,32,512]{2,0,1:T(2,128)}), f32[2,512,512]{2,0,1:T(2,128)}) %all-gather.6.cloned.1.call-update) | async-done | bytes 2097168 | tf_op jit(solution)/shard_map/all_gather | solution.py:40
  405.5 2.5 constant_dynamic-slice_fusion.1
  408.0 1.3 copy.21
  409.3 10.3 fusion.17
  419.6 13.9 %fusion.2 = f32[512,512,1]{1,0,2:T(8,128)S(1)} fusion(f32[4,512,512]{2,1,0:T(8,128)S(1)} %copy-done.1, f32[512,4,512]{2,0,1:T(8,128)S(1)} %fusion.17), kind=kOutput, calls=%fused_computation.2 | convolution fusion | flops 6442450944 | bytes 9437184 | tf_op jit(solution)/shard_map/pmk,pnk->mn/dot_general | solution.py:43
  433.5 19.3 %all_to_all.16 = f32[16,32,512]{2,1,0:T(8,128)S(1)} all-to-all(f32[16,32,512]{2,1,0:T(8,128)S(1)} %bitcast.76), channel_id=1, replica_groups=mesh['sec'=16,'op'=16] {'op'}, dimensions={0} | all-to-all | bytes 2097152 | tf_op jit(solution)/shard_map/all_to_all | solution.py:45
  452.8 1.6 fusion.9
  454.4 3.4 collective-permute-start.4
  457.7 3.8 collective-permute-done.4
  461.5 0.6 add.70
  462.1 1.4 collective-permute-start.5
  463.5 45.6 %collective-permute-done.5 = f32[32,32,512]{2,0,1:T(8,128)S(1)} collective-permute-done((f32[32,32,512]{2,0,1:T(8,128)S(1)}, f32[32,32,512]{2,0,1:T(8,128)S(1)}, u32[]{:S(2)}, u32[]{:S(2)}) %collective-permute-start.5) | collective-permute-done | bytes 2097184 | tf_op jit(solution)/shard_map/ppermute | solution.py:14
  509.1 0.6 add.71
  509.7 2.4 collective-permute-start.6
  512.1 90.1 %collective-permute-done.6 = f32[32,32,512]{2,0,1:T(8,128)S(1)} collective-permute-done((f32[32,32,512]{2,0,1:T(8,128)S(1)}, f32[32,32,512]{2,0,1:T(8,128)S(1)}, u32[]{:S(2)}, u32[]{:S(2)}) %collective-permute-start.6) | collective-permute-done | bytes 2097184 | tf_op jit(solution)/shard_map/ppermute | solution.py:14
  602.1 0.6 add.72
  602.8 6.5 collective-permute-start.7
  609.3 90.7 %collective-permute-done.7 = f32[32,32,512]{2,0,1:T(8,128)S(1)} collective-permute-done((f32[32,32,512]{2,0,1:T(8,128)S(1)}, f32[32,32,512]{2,0,1:T(8,128)S(1)}, u32[]{:S(2)}, u32[]{:S(2)}) %collective-permute-start.7) | collective-permute-done | bytes 2097184 | tf_op jit(solution)/shard_map/ppermute | solution.py:14
  700.0 0.9 fusion.22
  701.0 45.1 %all-gather.8.cloned.1.call-done = f32[2,512,512]{2,0,1:T(2,128)} async-done(((f32[2,32,512]{2,0,1:T(2,128)}), f32[2,512,512]{2,0,1:T(2,128)}) %all-gather.8.cloned.1.call-update) | async-done | bytes 2097168 | tf_op jit(solution)/shard_map/all_gather | solution.py:40
  746.1 2.5 constant_dynamic-slice_fusion
  748.6 1.3 copy.24
  749.9 10.2 fusion.15
  760.2 13.7 %fusion = f32[512,512,1]{1,0,2:T(8,128)S(1)} fusion(f32[4,512,512]{2,1,0:T(8,128)S(1)} %copy-done.2, f32[512,4,512]{2,0,1:T(8,128)S(1)} %fusion.15), kind=kOutput, calls=%fused_computation | convolution fusion | flops 6442450944 | bytes 9437184 | tf_op jit(solution)/shard_map/pmk,pnk->mn/dot_general | solution.py:43
  773.9 19.3 %all_to_all.17 = f32[16,32,512]{2,1,0:T(8,128)S(1)} all-to-all(f32[16,32,512]{2,1,0:T(8,128)S(1)} %bitcast.77), channel_id=1, replica_groups=mesh['sec'=16,'op'=16] {'op'}, dimensions={0} | all-to-all | bytes 2097152 | tf_op jit(solution)/shard_map/all_to_all | solution.py:45
  793.2 1.6 fusion.6
  794.7 3.3 collective-permute-start.8
  798.1 3.8 collective-permute-done.8
  801.9 0.6 add.74
  802.5 1.4 collective-permute-start.9
  803.9 45.6 %collective-permute-done.9 = f32[32,32,512]{2,0,1:T(8,128)S(1)} collective-permute-done((f32[32,32,512]{2,0,1:T(8,128)S(1)}, f32[32,32,512]{2,0,1:T(8,128)S(1)}, u32[]{:S(2)}, u32[]{:S(2)}) %collective-permute-start.9) | collective-permute-done | bytes 2097184 | tf_op jit(solution)/shard_map/ppermute | solution.py:14
  849.4 0.6 add.75
  850.1 2.4 collective-permute-start.10
  852.4 90.1 %collective-permute-done.10 = f32[32,32,512]{2,0,1:T(8,128)S(1)} collective-permute-done((f32[32,32,512]{2,0,1:T(8,128)S(1)}, f32[32,32,512]{2,0,1:T(8,128)S(1)}, u32[]{:S(2)}, u32[]{:S(2)}) %collective-permute-start.10) | collective-permute-done | bytes 2097184 | tf_op jit(solution)/shard_map/ppermute | solution.py:14
  942.5 0.6 add.76
  943.1 6.5 collective-permute-start.11
  949.7 0.7 copy.28
  950.3 90.0 %collective-permute-done.11 = f32[32,32,512]{2,0,1:T(8,128)S(1)} collective-permute-done((f32[32,32,512]{2,0,1:T(8,128)S(1)}, f32[32,32,512]{2,0,1:T(8,128)S(1)}, u32[]{:S(2)}, u32[]{:S(2)}) %collective-permute-start.11) | collective-permute-done | bytes 2097184 | tf_op jit(solution)/shard_map/ppermute | solution.py:14
  1040.4 0.2 fusion.24
  1040.6 0.7 copy.27
  (20 shorter events, 0.2 us)
Async XLA Ops:
  7.2 56.8 %all-gather.4.cloned.1.call-start = ((), (), s32[]{:S(2)}) async-start(), calls=%async_computation.3 | async-start | bytes 2228224 | tf_op jit(solution)/shard_map/all_gather | solution.py:40
  10.4 395.0 %all-gather.6.cloned.1.call-start = ((), (), s32[]{:S(2)}) async-start(), calls=%async_computation.4 | async-start | bytes 2228224 | tf_op jit(solution)/shard_map/all_gather | solution.py:40
  67.8 10.6 %copy-start = (f32[4,512,512]{2,1,0:T(8,128)S(1)}, f32[4,512,512]{2,1,0:T(8,128)}, u32[]{:S(2)}) copy-start(f32[4,512,512]{2,1,0:T(8,128)} %param.11) | copy-start | bytes 12582916
  92.0 19.3 %copy-start.6 = (s32[16]{0:T(128)S(1)}, s32[16]{0:T(128)}, u32[]{:S(2)}) copy-start(s32[16]{0:T(128)} %param.9) | copy-start | bytes 196
  112.9 7.1 collective-permute-start
  120.7 46.9 %collective-permute-start.1 = (f32[32,32,512]{2,0,1:T(8,128)S(1)}, f32[32,32,512]{2,0,1:T(8,128)S(1)}, u32[]{:S(2)}, u32[]{:S(2)}) collective-permute-start(f32[32,32,512]{2,0,1:T(8,128)S(1)} %add.65), channel_id=1, source_target_pairs={{0,32},{16,48},{32,0},{48,16},{64,96},{80,112},{96,64},{112,80},{1... | collective-permute-start | bytes 6291464 | tf_op jit(solution)/shard_map/ppermute | solution.py:14
  168.2 92.4 %collective-permute-start.2 = (f32[32,32,512]{2,0,1:T(8,128)S(1)}, f32[32,32,512]{2,0,1:T(8,128)S(1)}, u32[]{:S(2)}, u32[]{:S(2)}) collective-permute-start(f32[32,32,512]{2,0,1:T(8,128)S(1)} %add.66), channel_id=1, source_target_pairs={{0,64},{16,80},{32,96},{48,112},{64,0},{80,16},{96,32},{112,48},{1... | collective-permute-start | bytes 6291464 | tf_op jit(solution)/shard_map/ppermute | solution.py:14
  261.1 97.3 %collective-permute-start.3 = (f32[32,32,512]{2,0,1:T(8,128)S(1)}, f32[32,32,512]{2,0,1:T(8,128)}, u32[]{:S(2)}, u32[]{:S(2)}) collective-permute-start(f32[32,32,512]{2,0,1:T(8,128)S(1)} %add.67), channel_id=1, source_target_pairs={{0,128},{16,144},{32,160},{48,176},{64,192},{80,208},{96,224},{112... | collective-permute-start | bytes 6291464 | tf_op jit(solution)/shard_map/ppermute | solution.py:14
  360.3 385.7 %all-gather.8.cloned.1.call-start = ((), (), s32[]{:S(2)}) async-start(), calls=%async_computation.5 | async-start | bytes 2228224 | tf_op jit(solution)/shard_map/all_gather | solution.py:40
  409.3 10.3 copy-start.1
  454.4 7.1 collective-permute-start.4
  462.1 46.9 %collective-permute-start.5 = (f32[32,32,512]{2,0,1:T(8,128)S(1)}, f32[32,32,512]{2,0,1:T(8,128)S(1)}, u32[]{:S(2)}, u32[]{:S(2)}) collective-permute-start(f32[32,32,512]{2,0,1:T(8,128)S(1)} %add.70), channel_id=1, source_target_pairs={{0,32},{16,48},{32,0},{48,16},{64,96},{80,112},{96,64},{112,80},{1... | collective-permute-start | bytes 6291464 | tf_op jit(solution)/shard_map/ppermute | solution.py:14
  509.7 190.3 %copy-start.5 = (f32[2,32,512]{2,1,0:T(8,128)S(1)}, f32[2,32,512]{2,1,0:T(8,128)}, u32[]{:S(2)}) copy-start(f32[2,32,512]{2,1,0:T(8,128)} %param.6) | copy-start | bytes 393220
  509.7 92.4 %collective-permute-start.6 = (f32[32,32,512]{2,0,1:T(8,128)S(1)}, f32[32,32,512]{2,0,1:T(8,128)S(1)}, u32[]{:S(2)}, u32[]{:S(2)}) collective-permute-start(f32[32,32,512]{2,0,1:T(8,128)S(1)} %add.71), channel_id=1, source_target_pairs={{0,64},{16,80},{32,96},{48,112},{64,0},{80,16},{96,32},{112,48},{1... | collective-permute-start | bytes 6291464 | tf_op jit(solution)/shard_map/ppermute | solution.py:14
  602.8 97.3 %collective-permute-start.7 = (f32[32,32,512]{2,0,1:T(8,128)S(1)}, f32[32,32,512]{2,0,1:T(8,128)S(1)}, u32[]{:S(2)}, u32[]{:S(2)}) collective-permute-start(f32[32,32,512]{2,0,1:T(8,128)S(1)} %add.72), channel_id=1, source_target_pairs={{0,128},{16,144},{32,160},{48,176},{64,192},{80,208},{96,224},{112... | collective-permute-start | bytes 6291464 | tf_op jit(solution)/shard_map/ppermute | solution.py:14
  749.9 10.3 copy-start.2
  794.7 7.1 collective-permute-start.8
  802.5 46.9 %collective-permute-start.9 = (f32[32,32,512]{2,0,1:T(8,128)S(1)}, f32[32,32,512]{2,0,1:T(8,128)S(1)}, u32[]{:S(2)}, u32[]{:S(2)}) collective-permute-start(f32[32,32,512]{2,0,1:T(8,128)S(1)} %add.74), channel_id=1, source_target_pairs={{0,32},{16,48},{32,0},{48,16},{64,96},{80,112},{96,64},{112,80},{1... | collective-permute-start | bytes 6291464 | tf_op jit(solution)/shard_map/ppermute | solution.py:14
  850.1 99.6 %copy-start.4 = (f32[2,32,512]{2,0,1:T(2,128)S(1)}, f32[2,32,512]{2,0,1:T(2,128)}, u32[]{:S(2)}) copy-start(f32[2,32,512]{2,0,1:T(2,128)} %fusion.22) | copy-start | bytes 393220
  850.1 190.3 %copy-start.3 = (f32[2,32,512]{2,0,1:T(2,128)S(1)}, f32[2,32,512]{2,0,1:T(2,128)}, u32[]{:S(2)}) copy-start(f32[2,32,512]{2,0,1:T(2,128)} %and_select_fusion.2) | copy-start | bytes 393220
  850.1 92.4 %collective-permute-start.10 = (f32[32,32,512]{2,0,1:T(8,128)S(1)}, f32[32,32,512]{2,0,1:T(8,128)S(1)}, u32[]{:S(2)}, u32[]{:S(2)}) collective-permute-start(f32[32,32,512]{2,0,1:T(8,128)S(1)} %add.75), channel_id=1, source_target_pairs={{0,64},{16,80},{32,96},{48,112},{64,0},{80,16},{96,32},{112,48},{1... | collective-permute-start | bytes 6291464 | tf_op jit(solution)/shard_map/ppermute | solution.py:14
  943.1 97.2 %collective-permute-start.11 = (f32[32,32,512]{2,0,1:T(8,128)S(1)}, f32[32,32,512]{2,0,1:T(8,128)S(1)}, u32[]{:S(2)}, u32[]{:S(2)}) collective-permute-start(f32[32,32,512]{2,0,1:T(8,128)S(1)} %add.76), channel_id=1, source_target_pairs={{0,128},{16,144},{32,160},{48,176},{64,192},{80,208},{96,224},{112... | collective-permute-start | bytes 6291464 | tf_op jit(solution)/shard_map/ppermute | solution.py:14
Sparse Core Ops, SparseCore 0:
  11.0 52.8 all-gather.3
  360.5 44.9 all-gather.5
  701.1 44.9 all-gather.7
